TPU v7x, 512 devices: a whole 4x4x16 slice. The times are simulated.
512 devices in a mesh: dp: 8 (over x, core), expert: 64 (over y, z).
Axes of the slice: x: 4, y: 4, z: 16, core: 2. Of those that a mesh axis runs over, the one named last changes fastest.
Arguments:
- tokens_in: bfloat16 [65536, 3584], P(('dp', 'expert')), may hold values from -6 to 6
- out_grad: bfloat16 [65536, 3584], P(('dp', 'expert')), may hold values from -0.59765625 to 0.59765625
- router_logits: float32 [65536, 192], P(('dp', 'expert')), may hold values from -12 to 250
- expert_ids: int32 [65536, 8], P(('dp', 'expert')), may hold values from 0 to 191, all different within a row; in each aligned block of 128 rows (0 to 127, 128 to 255, ...) at most 8 rows name the same one
- saved_hidden: bfloat16 [8, 64, 64, 8, 1024], P('dp', 'expert'), may hold values from -6 to 6
- down_weight: bfloat16 [64, 1024, 3584], P('expert', 'dp'), may hold values from -0.1875 to 0.1875
Outputs:
- hidden_grad: bfloat16 [8, 64, 64, 8, 1024], P('dp', 'expert')
- logit_grad: float32 [65536, 192], P(('dp', 'expert'))
- router_grad: float32 [3584, 192], P('expert', 'dp')
Inputs may be any that keep to these rules, and one draw needn't show every extreme that they name: `expert_ids`: among the 128 rows of one device no expert is named by more than 8 rows, a bound that some block reaches.
All inputs are finite; a program needn't handle non-finite values.
Results may differ from a plain program's by a relative error of at most 0.013.
Values may be sent and summed in bfloat16 or wider, within the bound.
A program may use at most 64 MiB of HBM per device.

v0:
```python
import jax
import jax.numpy as jnp
from jax import lax
from jax.sharding import PartitionSpec as P

RSCALE = 2.827
ZLOSS = 0.25


def entering(shard, axis, combine, identity):
    length, place = (lax.axis_size(axis), lax.axis_index(axis))
    everything = lax.all_gather(shard.astype(jnp.bfloat16), axis)
    start = jnp.broadcast_to(jnp.asarray(identity, shard.dtype), shard.shape)

    def lap(k, before):
        reached = k < place
        new = combine(before, everything[k].astype(shard.dtype))
        return jnp.where(reached, new, before)

    return lax.fori_loop(0, length, lap, start)


def from_root(value, axis, source):
    kept = jnp.where(lax.axis_index(axis) == source, value, 0).astype(value.dtype)
    return lax.psum(kept, axis)


def slot_table(ids_block, flight, cap):
    owners = jnp.arange(flight, dtype=jnp.int32)
    chosen = jnp.any(ids_block[:, :, None] == owners[None, None, :], axis=1)
    as_int = chosen.astype(jnp.int32)
    rank = jnp.cumsum(as_int, axis=0) - as_int
    places = jnp.arange(cap, dtype=jnp.int32)
    table = chosen[None, :, :] & (rank[None, :, :] == places[:, None, None])
    return jnp.transpose(table, (2, 0, 1))


def own_columns(panel):
    count = panel.shape[1] // lax.axis_size("dp")
    return lax.dynamic_slice_in_dim(panel, lax.axis_index("dp") * count, count, 1)


def local(tokens_in, out_grad, router_logits, expert_ids, saved_hidden, down_weight):
    highest = lax.Precision.HIGHEST
    flight = lax.axis_size("expert")
    cap = saved_hidden.shape[3]
    hidden = saved_hidden.shape[4]
    width = out_grad.shape[1]
    experts = router_logits.shape[1]
    top = jnp.max(router_logits, axis=1, keepdims=True)
    shifted = jnp.exp(router_logits - top)
    total = jnp.sum(shifted, axis=1, keepdims=True)
    probs = shifted / total
    lse = top + jnp.log(total)
    columns = jnp.arange(experts, dtype=jnp.int32)
    picks = (expert_ids[:, :, None] == columns[None, None, :]).astype(jnp.float32)
    chosen_logit = jnp.sum(picks * router_logits[:, None, :], axis=2)
    scores = jax.nn.sigmoid(chosen_logit)
    ssum = jnp.sum(scores, axis=1, keepdims=True)
    gates = RSCALE * scores / ssum
    gate_half = gates.astype(jnp.bfloat16)
    in_window = picks[:, :, :flight]
    gate_te = jnp.sum(in_window * gate_half.astype(jnp.float32)[:, :, None], axis=1)
    table = slot_table(expert_ids, flight, cap)
    table_half = table.astype(jnp.bfloat16)
    table_full = table.astype(jnp.float32)
    send_rows = jnp.einsum(
        "ect,td->ecd", table_half, out_grad, preferred_element_type=jnp.float32
    ).astype(jnp.bfloat16)
    send_gates = jnp.einsum("ect,te->ec", table_full, gate_te, precision=highest).astype(
        jnp.bfloat16
    )
    recv_rows, recv_gates = (
        lax.all_to_all(send_rows, "expert", split_axis=0, concat_axis=0, tiled=True),
        lax.all_to_all(send_gates, "expert", split_axis=0, concat_axis=0, tiled=True),
    )
    flat_rows = recv_rows.reshape(flight * cap, width)
    part = lax.dot_general(
        flat_rows,
        lax.all_gather(down_weight, "dp", axis=1, tiled=True)[0],
        (((1,), (1,)), ((), ())),
        preferred_element_type=jnp.float32,
    )
    slot_gates = recv_gates.reshape(flight * cap, 1).astype(jnp.float32)
    hidden_grad = (slot_gates * part).astype(jnp.bfloat16).reshape(1, 1, flight, cap, hidden)
    saved_flat = saved_hidden.reshape(flight * cap, hidden)
    gate_grad = jnp.sum(saved_flat * part, axis=1).reshape(flight, cap)
    returned = lax.all_to_all(gate_grad, "expert", split_axis=0, concat_axis=0, tiled=True)
    grad_te = jnp.einsum("ect,ec->te", table_full, returned, precision=highest)
    grad_choice = jnp.sum(in_window * grad_te[:, None, :], axis=2)
    mixed = jnp.sum(grad_choice * gates, axis=1, keepdims=True) / RSCALE
    dscore = RSCALE / ssum * (grad_choice - mixed)
    dchosen = dscore * scores * (1.0 - scores)
    logit_grad = jnp.sum(picks * dchosen[:, :, None], axis=1) + 2.0 * ZLOSS * lse * probs
    tokens_full = tokens_in.astype(jnp.float32)
    own_rows = lax.psum_scatter(
        lax.dot_general(tokens_full, logit_grad, (((0,), (0,)), ((), ())), precision=highest),
        "expert",
        scatter_dimension=0,
        tiled=True,
    )
    before = entering(
        own_rows, "dp", lambda earlier, later: earlier + later, jnp.zeros_like(own_rows)
    )
    finished = before + own_rows
    spread = from_root(finished.astype(jnp.bfloat16), "dp", lax.axis_size("dp") - 1).astype(
        finished.dtype
    )
    router_grad = own_columns(spread)
    return (hidden_grad, logit_grad, router_grad)


def solution(mesh):
    in_specs = (
        P(("dp", "expert"), None),
        P(("dp", "expert"), None),
        P(("dp", "expert"), None),
        P(("dp", "expert"), None),
        P("dp", "expert", None, None, None),
        P("expert", "dp", None),
    )
    out_specs = (P("dp", "expert", None, None, None), P(("dp", "expert"), None), P("expert", "dp"))
    return jax.shard_map(local, mesh=mesh, in_specs=in_specs, out_specs=out_specs, check_vma=False)
```

profile of v0, /device:TPU:8, one launch (start us, length us, event | category | flops | bytes accessed | tf_op | source)
XLA Modules:
  0.0 974.6 jit_solution(7703707765535747499)
XLA Ops:
  7.2 0.8 fusion.6
  8.5 3.0 convolution_convert_fusion
  11.5 19.0 %all-to-all-start.1 = ((bf16[64,8,3584]{2,1,0:T(8,128)(2,1)}), bf16[64,8,3584]{2,1,0:T(8,128)(2,1)}, u32[]{:S(2)}, u32[]{:S(2)}) async-start(bf16[64,8,3584]{2,1,0:T(8,128)(2,1)} %convolution_convert_fusion), calls=%async_computation.1 | async-start | bytes 7340032 | tf_op jit(solution)/shard_map/all_to_all | solution.py:74
  30.6 0.7 all-gather.3.cloned.1.call-update
  31.7 55.6 %all-gather.3.cloned.1.call-done = bf16[1,1024,3584]{2,1,0:T(8,128)(2,1)} async-done(((bf16[1,128,3584]{2,1,0:T(8,128)(2,1)}), bf16[1,1024,3584]{2,1,0:T(8,128)(2,1)}) %all-gather.3.cloned.1.call-update) | async-done | bytes 7340048 | tf_op jit(solution)/shard_map/all_gather | solution.py:80
  87.3 106.5 %all-to-all-done.1 = bf16[64,8,3584]{2,1,0:T(8,128)(2,1)} async-done(((bf16[64,8,3584]{2,1,0:T(8,128)(2,1)}), bf16[64,8,3584]{2,1,0:T(8,128)(2,1)}, u32[]{:S(2)}, u32[]{:S(2)}) %all-to-all-start.1) | async-done | bytes 3670048 | tf_op jit(solution)/shard_map/all_to_all | solution.py:74
  193.8 8.4 fusion.3
  202.2 0.7 all_to_all.20
  202.9 9.7 all-to-all-start.2
  212.7 13.4 %all-to-all-done.2 = f32[64,1,8]{2,1,0:T(1,128)S(1)} async-done(((f32[64,1,8]{2,1,0:T(1,128)}), f32[64,1,8]{2,1,0:T(1,128)S(1)}, u32[]{:S(2)}, u32[]{:S(2)}) %all-to-all-start.2) | async-done | bytes 2080 | tf_op jit(solution)/shard_map/all_to_all | solution.py:88
  226.1 0.4 fusion.8
  226.7 4.0 convolution_bitcast_fusion
  230.7 4.7 copy.61
  235.5 0.4 fusion.11
  235.9 0.7 copy.52
  236.6 5.5 all-to-all-start
  242.1 13.5 %all-to-all-done = bf16[64,1,8]{2,1,0:T(2,128)(2,1)S(1)} async-done(((bf16[64,1,8]{2,1,0:T(2,128)(2,1)}), bf16[64,1,8]{2,1,0:T(2,128)(2,1)S(1)}, u32[]{:S(2)}, u32[]{:S(2)}) %all-to-all-start) | async-done | bytes 1056 | tf_op jit(solution)/shard_map/all_to_all | solution.py:75
  255.9 1.2 fusion.4
  257.0 668.6 %reduce-scatter.4.cloned.1.call-done = f32[56,192]{1,0:T(8,128)} async-done(((f32[3584,192]{1,0:T(8,128)}), f32[56,192]{1,0:T(8,128)}) %reduce-scatter.4.cloned.1.call-update) | async-done | bytes 43024 | tf_op jit(solution)/shard_map/reduce_scatter | solution.py:96
  925.6 0.8 convert_element_type.90
  926.4 13.2 %all-gather = bf16[448,192]{1,0:T(8,128)(2,1)S(1)} all-gather(bf16[56,192]{1,0:T(8,128)(2,1)S(1)} %convert_element_type.90), channel_id=2, replica_groups=mesh['dp'=8,'expert'=64] {'dp'}, dimensions={0}, use_global_device_ids=true | all-gather | bytes 193536 | tf_op jit(solution)/shard_map/all_gather | solution.py:12
  940.1 0.9 copy.62
  941.0 26.1 %psum.7 = bf16[56,192]{0,1:T(8,128)(2,1)S(1)} all-reduce(bf16[56,192]{0,1:T(8,128)(2,1)S(1)} %fusion.20), channel_id=1, replica_groups=mesh['dp'=8,'expert'=64] {'dp'}, use_global_device_ids=true, to_apply=%region_14.15 | all-reduce | flops 10752 | bytes 43008 | tf_op jit(solution)/shard_map/psum | solution.py:25
  967.2 0.6 dynamic-slice_convert_fusion
  (46 shorter events, 2.0 us)
Async XLA Ops:
  7.2 1.3 copy-start
  11.5 19.8 %copy-start.1 = (f32[128,192]{0,1:T(8,128)S(1)}, f32[128,192]{0,1:T(8,128)}, u32[]{:S(2)}) copy-start(f32[128,192]{0,1:T(8,128)} %param.10) | copy-start | bytes 294916
  11.5 19.8 %copy-start.3 = (s32[128,8]{0,1:T(8,128)S(1)}, s32[128,8]{0,1:T(8,128)}, u32[]{:S(2)}) copy-start(s32[128,8]{0,1:T(8,128)} %param.11) | copy-start | bytes 12292
  11.5 182.3 %all-to-all-start.1 = ((bf16[64,8,3584]{2,1,0:T(8,128)(2,1)}), bf16[64,8,3584]{2,1,0:T(8,128)(2,1)}, u32[]{:S(2)}, u32[]{:S(2)}) async-start(bf16[64,8,3584]{2,1,0:T(8,128)(2,1)} %convolution_convert_fusion), calls=%async_computation.1 | async-start | bytes 7340032 | tf_op jit(solution)/shard_map/all_to_all | solution.py:74
  30.6 56.7 %all-gather.3.cloned.1.call-start = ((), (), s32[]{:S(2)}) async-start(), calls=%async_computation.4 | async-start | bytes 8257536 | tf_op jit(solution)/shard_map/all_gather | solution.py:80
  202.9 23.1 %all-to-all-start.2 = ((f32[64,1,8]{2,1,0:T(1,128)}), f32[64,1,8]{2,1,0:T(1,128)S(1)}, u32[]{:S(2)}, u32[]{:S(2)}) async-start(f32[64,1,8]{2,1,0:T(1,128)} %bitcast.12), calls=%async_computation.2 | async-start | bytes 65536 | tf_op jit(solution)/shard_map/all_to_all | solution.py:88
  212.6 713.0 %reduce-scatter.4.cloned.1.call-start = ((), (), s32[]{:S(2)}) async-start(), calls=%async_computation.5 | async-start | bytes 3727360 | tf_op jit(solution)/shard_map/reduce_scatter | solution.py:96
  226.7 8.7 copy-start.2
  236.6 19.0 %all-to-all-start = ((bf16[64,1,8]{2,1,0:T(2,128)(2,1)}), bf16[64,1,8]{2,1,0:T(2,128)(2,1)S(1)}, u32[]{:S(2)}, u32[]{:S(2)}) async-start(bf16[64,1,8]{2,1,0:T(2,128)(2,1)} %copy.52), calls=%async_computation | async-start | bytes 65536 | tf_op jit(solution)/shard_map/all_to_all | solution.py:75
Sparse Core Ops, SparseCore 0:
  33.5 53.7 all-gather.2
  235.6 689.9 reduce-scatter.3
where the time goes:
time: 975 us
  waiting for transfers between devices  858 us (88%)
  blocking collectives  39.4 us (4%)
  starting transfers between devices  34.3 us (4%)
  matrix products  16.1 us (2%)
  between operations  14.2 us (1%)
    reduce_scatter x1, waiting for transfers between devices, local(): lax.psum_scatter(lax.dot_general(tokens_full, logit_grad, (((0,), (0,)),...  669 us
    all_to_all x1, waiting for transfers between devices, local(): lax.all_to_all(send_rows, 'expert', split_axis=0, concat_axis=0, tiled=True)  107 us
    all_gather x1, waiting for transfers between devices, local(): lax.all_gather(down_weight, 'dp', axis=1, tiled=True)[0]  55.6 us
    psum x1, blocking collectives, from_root(): return lax.psum(kept, axis)  26.1 us
  transfers between devices with their start and end apart: 5, of which 5 were waited for; matrix products, arithmetic and copies ran while one was open for 0% of the time, Pallas kernels for 0%

commit v1 on v0

--- a/solution.py
+++ b/solution.py
@@ -5,6 +5,13 @@
 
 RSCALE = 2.827
 ZLOSS = 0.25
+
+
+def all_by_exchange(block, axis, along):
+    devices = lax.axis_size(axis)
+    blocks = jnp.stack([block for _ in range(devices)])
+    blocks = lax.all_to_all(blocks, axis, split_axis=0, concat_axis=0)
+    return jnp.concatenate(blocks, axis=along)
 
 
 def entering(shard, axis, combine, identity):
@@ -77,7 +84,7 @@
     flat_rows = recv_rows.reshape(flight * cap, width)
     part = lax.dot_general(
         flat_rows,
-        lax.all_gather(down_weight, "dp", axis=1, tiled=True)[0],
+        all_by_exchange(down_weight, "dp", 1)[0],
         (((1,), (1,)), ((), ())),
         preferred_element_type=jnp.float32,
     )

time: 975 us -> 1060 us (1.087)
  the two profiles are of different devices: /device:TPU:8 before, /device:TPU:64 now
where the time goes in v1:
time: 1060 us
  waiting for transfers between devices  936 us (88%)
  blocking collectives  39.4 us (4%)
  starting transfers between devices  39.1 us (4%)
  matrix products  16 us (2%)
  between operations  14.2 us (1%)
  local copies, waits for them, and re-layouts  12.6 us (1%)
    reduce_scatter x1, waiting for transfers between devices, local(): lax.psum_scatter(lax.dot_general(tokens_full, logit_grad, (((0,), (0,)),...  668 us
    all_to_all x1, waiting for transfers between devices, local(): lax.all_to_all(send_rows, 'expert', split_axis=0, concat_axis=0, tiled=True)  163 us
    all_to_all x1, waiting for transfers between devices, all_by_exchange(): blocks = lax.all_to_all(blocks, axis, split_axis=0, concat_axis=0)  79.9 us
    psum x1, blocking collectives, from_root(): return lax.psum(kept, axis)  26.3 us
  transfers between devices with their start and end apart: 5, of which 5 were waited for; matrix products, arithmetic and copies ran while one was open for 1% of the time, Pallas kernels for 0%

profile of v1, /device:TPU:64, one launch (start us, length us, event | category | flops | bytes accessed | tf_op | source)
XLA Modules:
  0.0 1061.0 jit_solution(16227078849551884136)
XLA Ops:
  7.2 4.9 stack.2
  12.1 5.0 all-to-all-start.2
  17.6 2.9 convolution_convert_fusion
  20.5 79.9 %all-to-all-done.2 = bf16[8,1,128,3584]{3,2,1,0:T(8,128)(2,1)} async-done(((bf16[8,1,128,3584]{3,2,1,0:T(8,128)(2,1)}), bf16[8,1,128,3584]{3,2,1,0:T(8,128)(2,1)}, u32[]{:S(2)}, u32[]{:S(2)}) %all-to-all-start.2) | async-done | bytes 7340064 | tf_op jit(solution)/shard_map/all_to_all | solution.py:13
  100.4 18.1 %all-to-all-start.1 = ((bf16[64,8,3584]{2,1,0:T(8,128)(2,1)}), bf16[64,8,3584]{2,1,0:T(8,128)(2,1)}, u32[]{:S(2)}, u32[]{:S(2)}) async-start(bf16[64,8,3584]{2,1,0:T(8,128)(2,1)} %convolution_convert_fusion), calls=%async_computation.1 | async-start | bytes 7340032 | tf_op jit(solution)/shard_map/all_to_all | solution.py:81
  118.9 162.8 %all-to-all-done.1 = bf16[64,8,3584]{2,1,0:T(8,128)(2,1)} async-done(((bf16[64,8,3584]{2,1,0:T(8,128)(2,1)}), bf16[64,8,3584]{2,1,0:T(8,128)(2,1)}, u32[]{:S(2)}, u32[]{:S(2)}) %all-to-all-start.1) | async-done | bytes 3670048 | tf_op jit(solution)/shard_map/all_to_all | solution.py:81
  281.7 8.4 fusion.2
  290.1 0.7 all_to_all.24
  290.8 9.6 all-to-all-start.3
  300.5 12.5 %all-to-all-done.3 = f32[64,1,8]{2,1,0:T(1,128)S(1)} async-done(((f32[64,1,8]{2,1,0:T(1,128)}), f32[64,1,8]{2,1,0:T(1,128)S(1)}, u32[]{:S(2)}, u32[]{:S(2)}) %all-to-all-start.3) | async-done | bytes 2080 | tf_op jit(solution)/shard_map/all_to_all | solution.py:95
  313.0 0.4 fusion.7
  313.6 4.0 convolution_bitcast_fusion
  317.6 4.7 copy.61
  322.3 0.4 fusion.10
  322.8 0.7 copy.52
  323.5 6.3 all-to-all-start
  329.9 12.6 %all-to-all-done = bf16[64,1,8]{2,1,0:T(2,128)(2,1)S(1)} async-done(((bf16[64,1,8]{2,1,0:T(2,128)(2,1)}), bf16[64,1,8]{2,1,0:T(2,128)(2,1)S(1)}, u32[]{:S(2)}, u32[]{:S(2)}) %all-to-all-start) | async-done | bytes 1056 | tf_op jit(solution)/shard_map/all_to_all | solution.py:82
  342.7 1.2 fusion.3
  343.8 668.1 %reduce-scatter.4.cloned.1.call-done = f32[56,192]{1,0:T(8,128)} async-done(((f32[3584,192]{1,0:T(8,128)}), f32[56,192]{1,0:T(8,128)}) %reduce-scatter.4.cloned.1.call-update) | async-done | bytes 43024 | tf_op jit(solution)/shard_map/reduce_scatter | solution.py:103
  1011.9 0.8 convert_element_type.90
  1012.7 13.2 %all-gather = bf16[448,192]{1,0:T(8,128)(2,1)S(1)} all-gather(bf16[56,192]{1,0:T(8,128)(2,1)S(1)} %convert_element_type.90), channel_id=2, replica_groups=mesh['dp'=8,'expert'=64] {'dp'}, dimensions={0}, use_global_device_ids=true | all-gather | bytes 193536 | tf_op jit(solution)/shard_map/all_gather | solution.py:19
  1026.3 0.9 copy.62
  1027.3 26.3 %psum.7 = bf16[56,192]{0,1:T(8,128)(2,1)S(1)} all-reduce(bf16[56,192]{0,1:T(8,128)(2,1)S(1)} %fusion.19), channel_id=1, replica_groups=mesh['dp'=8,'expert'=64] {'dp'}, use_global_device_ids=true, to_apply=%region_14.15 | all-reduce | flops 10752 | bytes 43008 | tf_op jit(solution)/shard_map/psum | solution.py:32
  1053.5 0.6 dynamic-slice_convert_fusion
  (46 shorter events, 2.0 us)
Async XLA Ops:
  7.2 10.5 copy-start
  12.1 5.0 copy-start.3
  12.1 88.4 %all-to-all-start.2 = ((bf16[8,1,128,3584]{3,2,1,0:T(8,128)(2,1)}), bf16[8,1,128,3584]{3,2,1,0:T(8,128)(2,1)}, u32[]{:S(2)}, u32[]{:S(2)}) async-start(bf16[8,1,128,3584]{3,2,1,0:T(8,128)(2,1)} %stack.2), calls=%async_computation.2 | async-start | bytes 14680064 | tf_op jit(solution)/shard_map/all_to_all | solution.py:13
  20.5 98.0 %copy-start.1 = (f32[128,192]{0,1:T(8,128)S(1)}, f32[128,192]{0,1:T(8,128)}, u32[]{:S(2)}) copy-start(f32[128,192]{0,1:T(8,128)} %param.10) | copy-start | bytes 294916
  100.4 181.2 %all-to-all-start.1 = ((bf16[64,8,3584]{2,1,0:T(8,128)(2,1)}), bf16[64,8,3584]{2,1,0:T(8,128)(2,1)}, u32[]{:S(2)}, u32[]{:S(2)}) async-start(bf16[64,8,3584]{2,1,0:T(8,128)(2,1)} %convolution_convert_fusion), calls=%async_computation.1 | async-start | bytes 7340032 | tf_op jit(solution)/shard_map/all_to_all | solution.py:81
  290.8 22.2 %all-to-all-start.3 = ((f32[64,1,8]{2,1,0:T(1,128)}), f32[64,1,8]{2,1,0:T(1,128)S(1)}, u32[]{:S(2)}, u32[]{:S(2)}) async-start(f32[64,1,8]{2,1,0:T(1,128)} %bitcast.13), calls=%async_computation.3 | async-start | bytes 65536 | tf_op jit(solution)/shard_map/all_to_all | solution.py:95
  300.5 711.4 %reduce-scatter.4.cloned.1.call-start = ((), (), s32[]{:S(2)}) async-start(), calls=%async_computation.5 | async-start | bytes 3727360 | tf_op jit(solution)/shard_map/reduce_scatter | solution.py:103
  313.6 8.7 copy-start.2
  323.5 19.0 %all-to-all-start = ((bf16[64,1,8]{2,1,0:T(2,128)(2,1)}), bf16[64,1,8]{2,1,0:T(2,128)(2,1)S(1)}, u32[]{:S(2)}, u32[]{:S(2)}) async-start(bf16[64,1,8]{2,1,0:T(2,128)(2,1)} %copy.52), calls=%async_computation | async-start | bytes 65536 | tf_op jit(solution)/shard_map/all_to_all | solution.py:82
Sparse Core Ops, SparseCore 0:
  322.5 689.3 reduce-scatter.3
